TPU v7x, 128 devices: a whole 4x4x4 slice. The times are simulated.
128 devices in a mesh: frame: 16 (over z_lo, x, core), mp: 8 (over z_hi, y).
Axes of the slice: x: 4, y: 4, z: 4 (z_hi: 2, z_lo: 2; z = z_hi * 2 + z_lo), core: 2. Of those that a mesh axis runs over, the one named last changes fastest.
Arguments:
- stream: bfloat16 [65536, 1408], P('frame'), may hold values from -6 to 6
- norm_gain: float32 [1408], replicated, may hold values from 0.1 to 1.9
- w_qkv: bfloat16 [3, 1408, 1408], P(None, None, 'mp'), may hold values from -1 to 1
- w_out: bfloat16 [1408, 1408], P('mp'), may hold values from -0.15625 to 0.15625
- pool_gain: float32 [1408], replicated, may hold values from 0.1 to 1.9
- w_llm: bfloat16 [1408, 4096], P(None, 'mp'), may hold values from -0.15625 to 0.15625
- owner_slot: int32 [16384], replicated, may hold values from 0 to 16383, as said below
Outputs:
- llm_rows: bfloat16 [16384, 4096], P('frame', 'mp')
Inputs may be any that keep to these rules, and one draw needn't show every extreme that they name: owner_slot is a permutation of the 16384 rows; the pooled rows of each aligned block of 1024 send exactly 64 rows into each aligned block of 1024 destinations.
All inputs are finite; a program needn't handle non-finite values.
Results may differ from a plain program's by a relative error of at most 0.009.
Values may be sent and summed in bfloat16 or wider, within the bound.
A program may use at most 128 MiB of HBM per device.

v0:
```python
import math

import jax
import jax.numpy as jnp
from jax import lax
from jax.sharding import PartitionSpec as P

HDIM = 88
FRAMES = 128
PATCHES = 256


def layer_norm(values, scale_gain):
    average = jnp.mean(values, axis=-1, keepdims=True)
    centered = values - average
    spread = jnp.mean(centered * centered, axis=-1, keepdims=True)
    return centered * lax.rsqrt(spread + 1e-06) * scale_gain


def per_device(stream, norm_gain, w_qkv, w_out, pool_gain, w_llm, owner_slot):
    own_index = lax.axis_index("frame")
    row_count = stream.shape[0]
    feature_width = stream.shape[1]
    local_width = w_qkv.shape[2]
    heads_here = local_width // HDIM
    frames_here = row_count // PATCHES
    pooled_rows = frames_here // 4 * PATCHES
    factor = 1.0 / math.sqrt(HDIM)
    wide_in = stream.astype(jnp.float32)
    normed = layer_norm(wide_in, norm_gain).astype(jnp.bfloat16)
    projections = jnp.einsum(
        "td,jde->jte", normed, w_qkv, preferred_element_type=jnp.float32
    ).astype(jnp.bfloat16)
    projections = projections.reshape(3, frames_here, PATCHES, heads_here, HDIM)
    incoming_block = lax.all_to_all(projections, "frame", split_axis=2, concat_axis=1, tiled=True)
    frame_rows = incoming_block.shape[1]
    patch_here = incoming_block.shape[2]
    items = incoming_block.shape[3]
    clips_all = frame_rows // FRAMES
    parts = incoming_block.reshape(3, clips_all, FRAMES, patch_here, items, HDIM)
    scores = (
        jnp.einsum("cfpke,cgpke->cpkfg", parts[0], parts[1], preferred_element_type=jnp.float32)
        * factor
    )
    probs = jax.nn.softmax(scores, axis=-1).astype(jnp.bfloat16)
    mixed = jnp.einsum(
        "cpkfg,cgpke->cfpke", probs, parts[2], preferred_element_type=jnp.float32
    ).astype(jnp.bfloat16)
    mixed = mixed.reshape(frame_rows, patch_here, items, HDIM)
    returned = lax.all_to_all(mixed, "frame", split_axis=0, concat_axis=1, tiled=True)
    returned = (
        returned.reshape(frames_here // 4, 4, PATCHES, heads_here, HDIM)
        .astype(jnp.float32)
        .mean(axis=1)
        .astype(jnp.bfloat16)
    )
    pooled_att = returned.reshape(pooled_rows, local_width)
    pooled_in = (
        wide_in.reshape(frames_here // 4, 4, PATCHES, feature_width)
        .mean(axis=1)
        .reshape(pooled_rows, feature_width)
    )
    partial_out = jnp.dot(pooled_att, w_out, preferred_element_type=jnp.float32)
    merged = pooled_in + lax.psum(partial_out, "mp")
    final = layer_norm(merged, pool_gain).astype(jnp.bfloat16)
    projected = jnp.dot(final, w_llm, preferred_element_type=jnp.float32).astype(jnp.bfloat16)
    everything = lax.all_gather(projected, "frame", axis=0, tiled=True)
    total_rows = everything.shape[0]
    source = (
        jnp.zeros((total_rows,), jnp.int32)
        .at[owner_slot]
        .set(jnp.arange(total_rows, dtype=jnp.int32))
    )
    my_sources = lax.dynamic_slice_in_dim(source, own_index * pooled_rows, pooled_rows)
    return everything[my_sources]


def solution(mesh):
    return jax.shard_map(
        per_device,
        mesh=mesh,
        in_specs=(
            P("frame", None),
            P(),
            P(None, None, "mp"),
            P("mp", None),
            P(),
            P(None, "mp"),
            P(),
        ),
        out_specs=P("frame", "mp"),
        check_vma=False,
    )
```

profile of v0, /device:TPU:1, one launch (start us, length us, event | category | flops | bytes accessed | tf_op | source)
XLA Modules:
  0.0 441.9 jit_solution(18287736248400874366)
XLA Ops:
  6.5 0.0 copy-start
  6.5 0.0 all-reduce.2.cloned.1.call-start
  6.5 6.0 %convert_reduce_fusion = f32[4096]{0:T(1024)S(1)} fusion(bf16[4096,1408]{1,0:T(8,128)(2,1)} %param.7), kind=kLoop, calls=%fused_computation.5 | loop fusion | flops 11530240 | bytes 11550720 | tf_op jit(solution)/shard_map/reduce_sum | solution.py:14
  12.5 0.0 copy-start.7
  12.5 7.4 %multiply_reduce_fusion = f32[4096]{0:T(1024)S(1)} fusion(bf16[4096,1408]{1,0:T(8,128)(2,1)} %param.7, f32[4096]{0:T(1024)S(1)} %broadcast_multiply_fusion.1), kind=kLoop, calls=%fused_computation.4 | loop fusion | flops 23064576 | bytes 11567104 | tf_op jit(solution)/shard_map/reduce_sum | solution.py:16
  20.0 0.0 copy-done
  20.0 0.0 copy-done.7
  20.0 10.0 %fusion.1 = f32[4096,528]{0,1:S(1)} fusion(bf16[1408,528]{0,1:T(8,128)(2,1)S(1)} %bitcast.42, bf16[4096,1408]{1,0:T(8,128)(2,1)} %param.7, f32[1408]{0:T(1024)S(1)} %copy-done.7, f32[4096]{0:T(1024)S(1)} %add_rsqrt_fusion, f32[4096]{0:T(1024)S(1)} %broadcast_multiply_fusion.1), kind=kOutput, calls=%fused_computation.6 | convolution fusion | flops 6118965248 | bytes 21710336
  30.0 0.6 convert_element_type.48
  30.6 3.5 copy.62
  34.2 11.6 %copy.44 = bf16[3,16,256,2,88]{4,3,1,0,2:T(2,128)(2,1)} copy(bf16[3,16,256,2,88]{2,1,4,3,0:T(8,128)(2,1)} %bitcast.46) | data formatting | bytes 8650752 | tf_op jit(solution)/shard_map/reshape | solution.py:34
  45.8 78.8 %all_to_all.24 = bf16[3,16,256,2,88]{4,3,1,0,2:T(2,128)(2,1)S(1)} all-to-all(bf16[3,16,256,2,88]{4,3,1,0,2:T(2,128)(2,1)} %copy.44), channel_id=1, replica_groups=mesh['frame'=16,'mp'=8] {'frame'}, dimensions={2} | all-to-all | bytes 8650752 | tf_op jit(solution)/shard_map/all_to_all | solution.py:35
  124.6 2.4 copy.45
  127.0 1.1 fusion.30
  128.2 0.5 copy.47
  128.7 0.5 copy.48
  129.3 2.4 fusion.14
  131.7 4.3 fusion.31
  136.0 0.5 copy.46
  136.5 1.9 fusion.22
  138.4 3.9 copy.60
  142.3 31.4 %all_to_all.25 = bf16[256,16,2,88]{3,2,1,0:T(2,128)(2,1)S(1)} all-to-all(bf16[256,16,2,88]{3,2,1,0:T(2,128)(2,1)} %bitcast.50), channel_id=1, replica_groups=mesh['frame'=16,'mp'=8] {'frame'}, dimensions={0} | all-to-all | bytes 2883584 | tf_op jit(solution)/shard_map/all_to_all | solution.py:50
  173.7 0.3 copy.55
  173.9 0.6 convert_bitcast_fusion
  174.5 2.5 copy.56
  177.0 2.8 reduce_sum.67
  179.8 0.3 copy.57
  180.1 0.1 multiply_convert_fusion.6
  180.2 0.2 copy.58
  180.4 0.0 copy-done.4
  180.4 3.6 fusion.32
  184.0 0.0 all-reduce.2.cloned.1.call-update
  184.1 0.0 all-gather.2.cloned.1.call-start
  184.1 9.0 %reduce_sum.63 = f32[4,256,1408]{2,1,0:T(8,128)} reduce(bf16[4,4,256,1408]{3,2,1,0:T(8,128)(2,1)} %bitcast.43, f32[]{:T(128)} %constant.11.clone.1), dimensions={1}, to_apply=%region_0.0 | reduce | flops 4325376 | bytes 17301508 | tf_op jit(solution)/shard_map/reduce_sum | solution.py:60
  193.1 5.5 %broadcast_multiply_fusion = f32[4,256,1408]{2,1,0:T(8,128)} fusion(f32[4,256,1408]{2,1,0:T(8,128)} %reduce_sum.63), kind=kLoop, calls=%fused_computation.22 | loop fusion | flops 1441792 | bytes 11534336 | tf_op jit(solution)/shard_map/div | solution.py:60
  198.6 122.0 %all-reduce.2.cloned.1.call-done = f32[1024,1408]{1,0:T(8,128)} async-done(((f32[1024,1408]{1,0:T(8,128)}), f32[1024,1408]{1,0:T(8,128)}) %all-reduce.2.cloned.1.call-update) | async-done | bytes 5767184 | tf_op jit(solution)/shard_map/psum | solution.py:64
  320.7 5.0 %fusion.29 = f32[1024]{0:T(1024)S(1)} fusion(f32[1024,1408]{1,0:T(8,128)} %all-reduce.2.cloned.1.call-done, f32[4,256,1408]{2,1,0:T(8,128)} %broadcast_multiply_fusion), kind=kLoop, calls=%fused_computation.43 | loop fusion | flops 2882560 | bytes 11538432 | tf_op jit(solution)/shard_map/reduce_sum | solution.py:14
  325.7 0.9 copy-done.2
  326.6 1.7 copy-done.3
  328.3 0.9 multiply_reduce_fusion.1
  329.2 0.4 copy-done.6
  329.7 0.0 copy-done.8
  329.7 2.9 fusion.21
  332.5 0.0 all-gather.2.cloned.1.call-update
  332.6 60.6 %scatter_custom_fusion = s32[16384]{0:T(1024)S(1)} fusion(s32[16384]{0:T(1024)S(1)} %compare_select_fusion, s32[16384]{0:T(1024)S(1)} %iota.3, s32[]{:T(128)} %constant.17.clone.1), kind=kCustom, calls=%fused_computation.34 | custom fusion | bytes 65540 | tf_op jit(solution)/shard_map/scatter | solution.py:72
  393.2 0.0 copy-start.1
  393.3 28.8 %all-gather.2.cloned.1.call-done = bf16[16384,512]{1,0:T(8,128)(2,1)} async-done(((bf16[1024,512]{1,0:T(8,128)(2,1)}), bf16[16384,512]{1,0:T(8,128)(2,1)}) %all-gather.2.cloned.1.call-update) | async-done | bytes 16777232 | tf_op jit(solution)/shard_map/all_gather | solution.py:67
  422.0 13.0 %gather_fusion = bf16[1024,512]{1,0:T(8,128)(2,1)} fusion(bf16[16384,512]{1,0:T(8,128)(2,1)} %all-gather.2.cloned.1.call-done, s32[1024]{0:T(1024)S(1)} %fusion.27), kind=kCustom, calls=%fused_computation | custom fusion | bytes 2101248 | tf_op jit(solution)/shard_map/gather | solution.py:75
  (16 shorter events, 0.1 us)
Async XLA Ops:
  6.5 13.4 %copy-start = (bf16[3,1408,176]{1,2,0:T(8,128)(2,1)S(1)}, bf16[3,1408,176]{1,2,0:T(8,128)(2,1)}, u32[]{:S(2)}) copy-start(bf16[3,1408,176]{1,2,0:T(8,128)(2,1)} %param.9) | copy-start | bytes 4460548
  6.5 314.1 %all-reduce.2.cloned.1.call-start = ((), (), s32[]{:S(2)}) async-start(), calls=%async_computation.2 | async-start | bytes 11534336 | tf_op jit(solution)/shard_map/psum | solution.py:64
  12.5 7.5 %copy-start.7 = (f32[1408]{0:T(1024)S(1)}, f32[1408]{0:T(1024)}, u32[]{:S(2)}) copy-start(f32[1408]{0:T(1024)} %param.8) | copy-start | bytes 16900
  177.0 3.4 copy-start.4
  184.1 238.0 %all-gather.2.cloned.1.call-start = ((), (), s32[]{:S(2)}) async-start(), calls=%async_computation.3 | async-start | bytes 17825792 | tf_op jit(solution)/shard_map/all_gather | solution.py:67
  320.6 6.0 %copy-start.2 = (f32[4,256,1408]{2,1,0:T(8,128)S(1)}, f32[4,256,1408]{2,1,0:T(8,128)}, u32[]{:S(2)}) copy-start(f32[4,256,1408]{2,1,0:T(8,128)} %broadcast_multiply_fusion) | copy-start | bytes 17301508
  320.7 7.7 %copy-start.3 = (f32[1024,1408]{1,0:T(8,128)S(1)}, f32[1024,1408]{1,0:T(8,128)}, u32[]{:S(2)}) copy-start(f32[1024,1408]{1,0:T(8,128)} %all-reduce.2.cloned.1.call-done) | copy-start | bytes 17301508
  328.3 1.4 copy-start.6
  328.3 1.4 copy-start.8
  329.7 2.9 copy-start.5
  393.2 41.8 %copy-start.1 = (bf16[3,1408,176]{1,2,0:T(8,128)(2,1)S(1)}, bf16[3,1408,176]{1,2,0:T(8,128)(2,1)}, u32[]{:S(2)}) copy-start(bf16[3,1408,176]{1,2,0:T(8,128)(2,1)} %param.9) | copy-start | bytes 4460548
Sparse Core Ops, SparseCore 0:
  184.2 136.4 all-reduce.1
  332.7 89.2 all-gather.1
where the time goes:
time: 443 us; the launch traced here: 442 us
  waiting for transfers between devices  151 us (34%)
  blocking collectives  110 us (25%)
  local copies, waits for them, and re-layouts  104 us (23%)
  other arithmetic  42.2 us (10%)
  matrix products  20.8 us (5%)
  between operations  13.6 us (3%)
    psum x1, waiting for transfers between devices, per_device(): merged = pooled_in + lax.psum(partial_out, 'mp')  122 us
    all_to_all x1, blocking collectives, per_device(): lax.all_to_all(projections, 'frame', split_axis=2, concat_axis=1, tiled=T...  78.8 us
    scatter x1, local copies, waits for them, and re-layouts, per_device(): source = jnp.zeros((total_rows,), jnp.int32).at[owner_slot].set(jnp.arang...  60.6 us
    all_to_all x1, blocking collectives, per_device(): lax.all_to_all(mixed, 'frame', split_axis=0, concat_axis=1, tiled=True)  31.4 us
    all_gather x1, waiting for transfers between devices, per_device(): everything = lax.all_gather(projected, 'frame', axis=0, tiled=True)  28.8 us
    gather x1, local copies, waits for them, and re-layouts, per_device(): return everything[my_sources]  13 us
    reshape x1, local copies, waits for them, and re-layouts, per_device(): projections = projections.reshape(3, frames_here, PATCHES, heads_here, HDIM)  11.6 us
    reduce_sum x2, other arithmetic, layer_norm(): average = jnp.mean(values, axis=-1, keepdims=True)  11 us
  transfers between devices with their start and end apart: 2, of which 2 were waited for; matrix products, arithmetic and copies ran while one was open for 17% of the time, Pallas kernels for 0%

commit v1 on v0

v1 whole, which is shorter than its diff:
```python
import functools
import math

import jax
import jax.numpy as jnp
from jax import lax
from jax.experimental import pallas as pl
from jax.experimental.pallas import tpu as pltpu
from jax.sharding import PartitionSpec as P

MESH = pl.DeviceIdType.MESH
NT = (((1,), (1,)), ((), ()))
HDIM = 88
D = 1408
W = 176
EPS = 1e-6
CHUNKS = 4
BF = jnp.bfloat16
F32 = jnp.float32


def iota(shape, dim):
    return lax.broadcasted_iota(jnp.int32, shape, dim)


def norm_rows(values, gain):
    average = jnp.mean(values, axis=-1, keepdims=True)
    centered = values - average
    spread = jnp.mean(centered * centered, axis=-1, keepdims=True)
    return centered * lax.rsqrt(spread + EPS) * gain


def kernel(
    x_ref, gain_ref, wt_ref, wout_ref, pgain_ref, wllm_ref, rank_ref, place_ref, out_ref,
    xb, nb, qsend, qrecv, tq, tk, tv, att, psend, arecv, wall, xs, fin, proj, fsend, frecv, perm, pool,
    xsem, xssem, qs_sem, qr_sem, ps_sem, pr_sem, ws_sem, wr_sem, wf_sem, wown_sem, fs_sem, fr_sem, os_sem, or_sem,
):
    f = lax.axis_index("frame")
    m = lax.axis_index("mp")
    clip8 = (f // 8) * 8
    j = f % 8
    cx = j // 2
    core = f % 2

    def mate(i):
        step = (1 + i % 3) * (1 - i // 6)
        return ((cx + step) % 4) * 2 + (core + i) % 2

    def source(i):
        step = (1 + i % 3) * (1 - i // 6)
        return ((cx + 4 - step) % 4) * 2 + (core + i) % 2

    def x_copy(i, slot):
        first = mate(i % 8) * 32 + (i // 8) * 16
        return pltpu.make_async_copy(x_ref.at[:, pl.ds(first, 16), :], xb.at[slot], xsem.at[slot])

    for i in range(2):
        x_copy(i, i).start()

    def xs_copy(half):
        return pltpu.make_async_copy(x_ref.at[:, pl.ds(m * 32 + half * 16, 16), :], xs.at[half], xssem.at[half])

    barrier = pltpu.get_barrier_semaphore()

    def greet(i, _):
        pl.semaphore_signal(barrier, inc=1, device_id=((f + i) % 16, m), device_id_type=MESH)
        return 0

    lax.fori_loop(1, 16, greet, 0)

    def greet_mp(i, _):
        pl.semaphore_signal(barrier, inc=1, device_id=(f, (m + i) % 8), device_id_type=MESH)
        return 0

    lax.fori_loop(1, 8, greet_mp, 0)

    def greet_back(i, _):
        @pl.when(jnp.logical_or(j != m, i != m))
        def _():
            pl.semaphore_signal(barrier, inc=1, device_id=(clip8 + m, i), device_id_type=MESH)

        return 0

    lax.fori_loop(0, 8, greet_back, 0)

    row, col = iota((128, 128), 0), iota((128, 128), 1)
    perm[...] = jnp.where((row >> 4 == (col & 7)) & ((row & 15) == col >> 3), 1.0, 0.0).astype(BF)
    row, col = iota((128, 512), 0), iota((128, 512), 1)
    hit = ((col >> 7) == ((row >> 2) & 3)) & (((col & 127) >> 2) == ((row >> 4) * 4 + (row & 3)))
    pool[...] = jnp.where(hit, 0.25, 0.0).astype(BF)
    tv[...] = jnp.where(iota((8, 128, 256), 2) == W, 1.0, 0.0).astype(BF)

    @pl.when(j == m)
    def _():
        pl.semaphore_wait(barrier, 29)

    @pl.when(j != m)
    def _():
        pl.semaphore_wait(barrier, 30)

    def w_copy(e):
        return pltpu.make_async_remote_copy(
            src_ref=wout_ref, dst_ref=wall.at[m], send_sem=ws_sem.at[e], recv_sem=wr_sem.at[e],
            device_id=(f, (m + e) % 8), device_id_type=MESH,
        )

    def w_pass(e):
        shard = wall.at[(m + 8 - e) % 8]
        return pltpu.make_async_remote_copy(
            src_ref=shard, dst_ref=shard, send_sem=ws_sem.at[e], recv_sem=wf_sem.at[e],
            device_id=(f + 1 - 2 * core, m), device_id_type=MESH,
        )

    def q_copy(i, half):
        to = mate(i % 8)
        chunk = (i // 8) * 2 + half
        return pltpu.make_async_remote_copy(
            src_ref=qsend.at[i, half], dst_ref=qrecv.at[chunk, j], send_sem=qs_sem.at[i, half],
            recv_sem=qr_sem.at[chunk, i % 8], device_id=(clip8 + to, m), device_id_type=MESH,
        )

    def q_own(i, half):
        chunk = (i // 8) * 2 + half
        return pltpu.make_async_copy(qsend.at[i, half], qrecv.at[chunk, j], qr_sem.at[chunk, 6])

    def q_start(i, half):
        @pl.when(i % 8 == 6)
        def _():
            q_own(i, half).start()

        @pl.when(i % 8 != 6)
        def _():
            q_copy(i, half).start()

    def project(i, _):
        slot = i % 2
        x_copy(i, slot).wait()

        def frames(t, _):
            y = norm_rows(xb[slot, pl.ds(2 * t, 2)].astype(F32).reshape(32, D), gain_ref[...])
            y = y.reshape(2, 2, 8, D)
            rows = pl.ds(pl.multiple_of(16 * t, 16), 16)
            nb[0, rows, :] = y[:, 0].reshape(16, D).astype(BF)
            nb[1, rows, :] = y[:, 1].reshape(16, D).astype(BF)
            return 0

        lax.fori_loop(0, 8, frames, 0, unroll=2)

        @pl.when(i + 2 < 16)
        def _():
            x_copy(i + 2, slot).start()

        qkv = lax.dot_general(wt_ref[...], nb[...].reshape(256, D), NT, preferred_element_type=F32)
        qsend[i, 0] = qkv[:, :128].astype(BF)
        qsend[i, 1] = qkv[:, 128:].astype(BF)
        q_start(i, 0)

        @pl.when(i < 8)
        def _():
            q_start(i, 1)

        return 0

    lax.fori_loop(0, 4, project, 0)
    own_w = pltpu.make_async_copy(wout_ref, wall.at[m], wown_sem)
    own_w.start()
    for half in range(2):
        xs_copy(half).start()
    for e in range(1, 8):

        @pl.when(core == e % 2)
        def _(e=e):
            w_copy(e).start()

    lax.fori_loop(4, 16, project, 0)

    def late(i, _):
        q_start(i, 1)
        return 0

    lax.fori_loop(8, 16, late, 0)

    def p_copy(chunk, i):
        to = (j + i) % 8
        rows = pl.ds(pl.multiple_of(chunk * 32, 32), 32)
        return pltpu.make_async_remote_copy(
            src_ref=psend.at[to, rows], dst_ref=arecv.at[m, rows], send_sem=ps_sem.at[chunk, i],
            recv_sem=pr_sem.at[chunk, m], device_id=(clip8 + to, j), device_id_type=MESH,
        )

    def p_own(chunk):
        rows = pl.ds(pl.multiple_of(chunk * 32, 32), 32)
        return pltpu.make_async_copy(psend.at[j, rows], arecv.at[m, rows], pr_sem.at[chunk, m])

    def attend(chunk):
        def turn(i, _):
            pltpu.make_async_copy(qsend.at[0, 0], qrecv.at[chunk, source(i)], qr_sem.at[chunk, i]).wait()
            s = source(i)
            block = qrecv.at[chunk, s]
            rows = pl.ds(pl.multiple_of(s * 16, 16), 16)
            for k, to in enumerate((tq, tk, tv)):
                part = lax.dot_general(perm[...], block[k * W : (k + 1) * W, :], NT, preferred_element_type=F32)
                to[:, rows, 0:W] = part.astype(BF).reshape(8, 16, W)
            return 0

        lax.fori_loop(0, 8, turn, 0)

        def quad(n, _):
            first = iota((128, W), 1) < HDIM
            wide = iota((128, 256), 1) < HDIM
            scale = math.log2(math.e) / math.sqrt(HDIM)
            for p in range(4):
                q = tq[4 * n + p]
                zero = jnp.zeros_like(q)
                q2 = jnp.concatenate([jnp.where(first, q, zero), jnp.where(first, zero, q)], axis=0)
                s = lax.dot_general(q2, tk[4 * n + p], NT, preferred_element_type=F32)
                top = jnp.max(s, axis=-1, keepdims=True)
                e = jnp.exp2((s - top) * scale).astype(BF)
                o = jnp.dot(e, tv[4 * n + p], preferred_element_type=F32)
                o = o * (1.0 / o[:, W : W + 1])
                att[p * 128 : (p + 1) * 128, :] = jnp.where(wide, o[:128], o[128:]).astype(BF)
            mean = jnp.dot(pool[...], att[...], preferred_element_type=F32).astype(BF)
            psend[:, pl.ds(pl.multiple_of(chunk * 32 + n * 16, 16), 16), :] = mean.reshape(8, 16, 256)
            return 0

        lax.fori_loop(0, 2, quad, 0)

        def back(i, _):
            here = jnp.logical_and(i == 0, j == m)

            @pl.when(here)
            def _():
                p_own(chunk).start()

            @pl.when(jnp.logical_not(here))
            def _():
                p_copy(chunk, i).start()

            return 0

        lax.fori_loop(0, 8, back, 0)

    def f_copy(chunk, e):
        rows = fin.at[m, pl.ds(pl.multiple_of(chunk * 32, 32), 32)]
        return pltpu.make_async_remote_copy(
            src_ref=rows, dst_ref=rows, send_sem=fs_sem.at[chunk, e], recv_sem=fr_sem.at[chunk, e],
            device_id=(f, (m + e) % 8), device_id_type=MESH,
        )

    def merge(chunk):
        rows = pl.ds(pl.multiple_of(chunk * 32, 32), 32)
        row, col = iota((32, 256), 0), iota((32, 256), 1)
        hit = ((col & 15) == (chunk % 2) * 8 + (row >> 2)) & ((col >> 6) == (row & 3))
        total = jnp.dot(
            jnp.where(hit, 0.25, 0.0).astype(BF), xs[chunk // 2].reshape(256, D), preferred_element_type=F32
        )
        for s in range(8):
            pltpu.make_async_copy(psend.at[0, rows], arecv.at[s, rows], pr_sem.at[chunk, s]).wait()
        for s in range(8):
            total += jnp.dot(arecv[s, rows, 0:W], wall[s], preferred_element_type=F32)
        fin[m, rows, :] = norm_rows(total, pgain_ref[...]).astype(BF)

        def spread(e, _):
            f_copy(chunk, e).start()
            return 0

        lax.fori_loop(1, 8, spread, 0)

    attend(0)
    for e in range(1, 8):

        @pl.when(core == e % 2)
        def _(e=e):
            w_copy(e).wait()
            w_pass(e).start()

    def middle(chunk, _):
        attend(chunk)

        @pl.when(chunk == 1)
        def _():
            own_w.wait()
            for half in range(2):
                xs_copy(half).wait()
            for e in range(1, 8):

                @pl.when(core == e % 2)
                def _(e=e):
                    w_pass(e).wait_send()

                @pl.when(core != e % 2)
                def _(e=e):
                    w_pass(e).wait_recv()

        merge(chunk - 1)
        return 0

    lax.fori_loop(1, CHUNKS, middle, 0)

    order = jnp.where(iota((1024, 1024), 0) == rank_ref[...], 1.0, 0.0).astype(BF)
    merge(CHUNKS - 1)

    def arrived(n, _):
        f_copy(n // 8, 1 + n % 8).wait_recv()
        return 0

    for chunk in range(CHUNKS):
        for e in range(1, 8):
            f_copy(chunk, e).wait_recv()

    def o_copy(half, i):
        to = (f + i) % 16
        return pltpu.make_async_remote_copy(
            src_ref=fsend.at[half, to], dst_ref=frecv.at[half, f], send_sem=os_sem.at[half, i],
            recv_sem=or_sem.at[half, i], device_id=(to, m), device_id_type=MESH,
        )

    for half in range(2):
        lanes = slice(half * 256, half * 256 + 256)
        for s in range(8):
            proj[s * 128 : (s + 1) * 128, :] = jnp.dot(
                fin[s], wllm_ref[:, lanes], preferred_element_type=F32
            ).astype(BF)
        turned = jnp.dot(order, proj[...], preferred_element_type=F32).astype(BF)
        fsend[half] = turned.reshape(16, 64, 256)

        def share(i, _, half=half):
            o_copy(half, i).start()
            return 0

        lax.fori_loop(1, 16, share, 0)
        frecv[half, f] = fsend[half, f]

    place = jnp.where(iota((1024, 1024), 0) == place_ref[...], 1.0, 0.0).astype(BF)
    for half in range(2):

        def landed(i, _, half=half):
            o_copy(half, i).wait_recv()
            return 0

        lax.fori_loop(1, 16, landed, 0)
        out_ref[:, half * 256 : half * 256 + 256] = jnp.dot(
            place, frecv[half].reshape(1024, 256), preferred_element_type=F32
        ).astype(BF)

    def left_q(i, _):
        @pl.when(i % 8 != 6)
        def _():
            q_copy(i, 0).wait_send()
            q_copy(i, 1).wait_send()

        return 0

    lax.fori_loop(0, 16, left_q, 0)

    def left_p(i, _):
        @pl.when(jnp.logical_not(jnp.logical_and(i == 0, j == m)))
        def _():
            for chunk in range(CHUNKS):
                p_copy(chunk, i).wait_send()

        return 0

    lax.fori_loop(0, 8, left_p, 0)

    def left_f(e, _):
        for chunk in range(CHUNKS):
            f_copy(chunk, e).wait_send()
        return 0

    lax.fori_loop(1, 8, left_f, 0)

    def left_o(i, _):
        for half in range(2):
            o_copy(half, i).wait_send()
        return 0

    lax.fori_loop(1, 16, left_o, 0)


def per_device(stream, norm_gain, w_qkv, w_out, pool_gain, w_llm, owner_slot):
    own = lax.axis_index("frame")
    frames = stream.reshape(16, 256, D)
    wt = jnp.swapaxes(w_qkv, 1, 2).reshape(3 * W, D)
    blocks = owner_slot.reshape(16, 1024)
    mine = lax.dynamic_index_in_dim(blocks, own, 0, keepdims=False)
    mine = mine.reshape(4, 256).T.reshape(1024)
    rank = jnp.sum((mine[:, None] < mine[None, :]).astype(jnp.int32), axis=0)[None]
    ordered = jnp.sort(blocks, axis=1)
    place = lax.dynamic_slice_in_dim(ordered, own * 64, 64, 1).reshape(1, 1024) - own * 1024
    vmem = pl.BlockSpec(memory_space=pltpu.VMEM)
    dma = pltpu.SemaphoreType.DMA
    return pl.pallas_call(
        kernel,
        out_shape=jax.ShapeDtypeStruct((1024, 512), BF),
        in_specs=[pl.BlockSpec(memory_space=pl.ANY)] + [vmem] * 7,
        out_specs=vmem,
        scratch_shapes=[
            pltpu.VMEM((2, 16, 16, D), BF),
            pltpu.VMEM((2, 128, D), BF),
            pltpu.VMEM((16, 2, 3 * W, 128), BF),
            pltpu.VMEM((4, 8, 3 * W, 128), BF),
            pltpu.VMEM((8, 128, W), BF),
            pltpu.VMEM((8, 128, W), BF),
            pltpu.VMEM((8, 128, 256), BF),
            pltpu.VMEM((512, 256), BF),
            pltpu.VMEM((8, 128, 256), BF),
            pltpu.VMEM((8, 128, 256), BF),
            pltpu.VMEM((8, W, D), BF),
            pltpu.VMEM((2, 16, 16, D), BF),
            pltpu.VMEM((8, 128, D), BF),
            pltpu.VMEM((1024, 256), BF),
            pltpu.VMEM((2, 16, 64, 256), BF),
            pltpu.VMEM((2, 16, 64, 256), BF),
            pltpu.VMEM((128, 128), BF),
            pltpu.VMEM((128, 512), BF),
            dma((2,)), dma((2,)), dma((16, 2)), dma((4, 8)), dma((4, 8)), dma((4, 8)),
            dma((8,)), dma((8,)), dma((8,)), dma, dma((4, 8)), dma((4, 8)), dma((2, 16)), dma((2, 16)),
        ],
        compiler_params=pltpu.CompilerParams(
            collective_id=0, has_side_effects=True, vmem_limit_bytes=56 * 2**20
        ),
        name="video_layer",
    )(frames, norm_gain[None], wt, w_out, pool_gain[None], w_llm, rank, place)


def solution(mesh):
    return jax.shard_map(
        per_device,
        mesh=mesh,
        in_specs=(
            P("frame", None), P(), P(None, None, "mp"), P("mp", None), P(), P(None, "mp"), P(),
        ),
        out_specs=P("frame", "mp"),
        check_vma=False,
    )
```

time: 443 us -> 150 us (0.34)
  waiting for transfers between devices: 151 us -> 0 us
  Pallas kernels: 0 us -> 125 us
  blocking collectives: 110 us -> 0 us
  local copies, waits for them, and re-layouts: 104 us -> 8.87 us
  other arithmetic: 42.2 us -> 1.84 us
  matrix products: 20.8 us -> 0 us
    pallas_call x0 -> x1, Pallas kernels: none -> 125 us  [per_device(): pl.pallas_call(kernel, out_shape=jax.ShapeDtypeStruct((1024, 512), BF), i...]
    psum x1 -> x0, waiting for transfers between devices: 122 us -> none  [per_device(): merged = pooled_in + lax.psum(partial_out, 'mp')]
    all_to_all x2 -> x0, blocking collectives: 110 us -> none  [the longest x1 78.8 us: per_device(): lax.all_to_all(projections, 'frame', split_axis=2, concat_axis=1, tiled=T...]
    scatter x1 -> x0, local copies, waits for them, and re-layouts: 60.6 us -> none  [per_device(): source = jnp.zeros((total_rows,), jnp.int32).at[owner_slot].set(jnp.arang...]
    reduce_sum x6 -> x1, other arithmetic: 31.1 us -> 1.07 us  [per_device(): jnp.sum((mine[:, None] < mine[None, :]).astype(jnp.int32), axis=0)[None]]
    all_gather x1 -> x0, waiting for transfers between devices: 28.8 us -> none  [per_device(): everything = lax.all_gather(projected, 'frame', axis=0, tiled=True)]
    reshape x2, local copies, waits for them, and re-layouts: 15.5 us -> 1.49 us  [the longest x1 1.48 us: per_device(): blocks = owner_slot.reshape(16, 1024)]
    gather x1 -> x0, local copies, waits for them, and re-layouts: 13 us -> none  [per_device(): return everything[my_sources]]
  transfers between devices with their start and end apart: 2 -> 0, of which waited for: 2 -> 0; matrix products, arithmetic and copies ran while one was open for 17% -> 0% of each run, Pallas kernels for 0% -> 0%
where the time goes in v1:
time: 150 us; the launch traced here: 149 us
  Pallas kernels  125 us (83%)
  between operations  13.4 us (9%)
  local copies, waits for them, and re-layouts  8.87 us (6%)
  other arithmetic  1.84 us (1%)
    pallas_call x1, Pallas kernels, per_device(): pl.pallas_call(kernel, out_shape=jax.ShapeDtypeStruct((1024, 512), BF), i...  125 us

profile of v1, /device:TPU:1, one launch (start us, length us, event | category | flops | bytes accessed | tf_op | source)
XLA Modules:
  0.0 149.5 jit_solution(11465505786254500298)
XLA Ops:
  6.5 0.0 sort.10.cloned.1.call-start
  6.5 1.5 reshape.32
  8.0 0.0 sort.10.cloned.1.call-update
  8.1 0.8 dynamic-slice_reduce_fusion
  8.8 0.1 copy.9
  9.0 0.1 lt.23
  9.1 1.1 convert_reduce_fusion
  10.2 1.3 broadcast_in_dim.9.gain_ref
  11.5 1.3 broadcast_in_dim.10.pgain_ref
  12.8 0.8 sort.10.cloned.1.call-done
  13.6 0.8 dynamic-slice_subtract_fusion
  14.3 0.7 sub.10.place_ref
  15.0 125.3 %video_layer.1 = bf16[1024,512]{1,0:T(8,128)(2,1)} custom-call(bf16[16,256,1408]{2,1,0:T(8,128)(2,1)} %bitcast.6, f32[1,1408]{1,0:T(1,128)} %broadcast_in_dim.9.gain_ref, bf16[528,1408]{1,0:T(8,128)(2,1)} %bitcast.7, bf16[176,1408]{1,0:T(8,128)(2,1)} %wout_ref.1, f32[1,1408]{1,0:T(1,128)} %broadcast_in_dim.10.pgain_ref, bf16[1408,512]{1,0:T(8,128)(2,1)} %wllm_ref.1, ...), custom_call_target="tpu_custom_call" | custom-call | tf_op jit(solution)/shard_map/video_layer/pallas_call | solution.py:393
  140.4 2.3 %copy.11 = bf16[1024,512]{1,0:T(8,128)(2,1)} copy(bf16[1024,512]{1,0:T(8,128)(2,1)} %video_layer.1) | data formatting | bytes 2097152
  (1 shorter events, 0.0 us)
Async XLA Ops:
  6.5 7.0 %sort.10.cloned.1.call-start = ((), (), s32[]{:S(2)}) async-start(), calls=%async_computation | async-start | bytes 196640 | tf_op jit(solution)/shard_map/jit(sort)/sort | solution.py:389
Sparse Core Ops, SparseCore 0:
  9.8 3.4 sort.12.cloned.1.call-done
  (1 shorter events, 0.0 us)

commit v2 on v1

v2 whole, which is shorter than its diff:
```python
import functools
import math

import jax
import jax.numpy as jnp
from jax import lax
from jax.experimental import pallas as pl
from jax.experimental.pallas import tpu as pltpu
from jax.sharding import PartitionSpec as P

MESH = pl.DeviceIdType.MESH
NT = (((1,), (1,)), ((), ()))
HDIM = 88
D = 1408
W = 176
EPS = 1e-6
CHUNKS = 4
FAR = sorted(((a, b, c) for a in (0, 1) for b in range(4) for c in (0, 1) if (a, b, c) != (0, 0, 0)), key=lambda s: -s[0] - min(s[1], 4 - s[1]))
BF = jnp.bfloat16
F32 = jnp.float32


def iota(shape, dim):
    return lax.broadcasted_iota(jnp.int32, shape, dim)


def norm_rows(values, gain):
    average = jnp.mean(values, axis=-1, keepdims=True)
    centered = values - average
    spread = jnp.mean(centered * centered, axis=-1, keepdims=True)
    return centered * lax.rsqrt(spread + EPS) * gain


def kernel(
    x_ref, gain_ref, wt_hbm, wout_hbm, pgain_ref, wllm_hbm, slot_ref, out_ref,
    wt_ref, wout_ref, wllm_ref, xb, nb0, nb1, qsend, qrecv, tq, tk, tv, att, psend, arecv, wall, xs, fin, proj, total, order, place, fsend, frecv, perm, pool,
    in_sem, xsem, xssem, qs_sem, qr_sem, ps_sem, pr_sem, ws_sem, wr_sem, wp_sem, wf_sem, wown_sem, fs_sem, fr_sem, os_sem, or_sem,
):
    f = lax.axis_index("frame")
    m = lax.axis_index("mp")
    clip8 = (f // 8) * 8
    j = f % 8
    cx = j // 2
    core = f % 2

    def mate(i):
        step = (1 + i % 3) * (1 - i // 6)
        return ((cx + step) % 4) * 2 + (core + i) % 2

    def source(i):
        step = (1 + i % 3) * (1 - i // 6)
        return ((cx + 4 - step) % 4) * 2 + (core + i) % 2

    def x_copy(i, slot):
        first = mate(i % 8) * 32 + (i // 8) * 16
        return pltpu.make_async_copy(x_ref.at[:, pl.ds(first, 16), :], xb.at[slot], xsem.at[slot])

    def w_in(n):
        ends = ((wt_hbm, wt_ref), (wout_hbm, wout_ref), (wllm_hbm, wllm_ref))[n]
        return pltpu.make_async_copy(*ends, in_sem.at[n])

    x_copy(0, 0).start()
    w_in(0).start()
    x_copy(1, 1).start()
    w_in(1).start()
    w_in(2).start()

    def xs_copy(half):
        return pltpu.make_async_copy(x_ref.at[:, pl.ds(m * 32 + half * 16, 16), :], xs.at[half], xssem.at[half])

    barrier = pltpu.get_barrier_semaphore()

    def greet(i, _):
        pl.semaphore_signal(barrier, inc=1, device_id=((f + i) % 16, m), device_id_type=MESH)
        return 0

    lax.fori_loop(1, 16, greet, 0)

    def greet_mp(i, _):
        pl.semaphore_signal(barrier, inc=1, device_id=(f, (m + i) % 8), device_id_type=MESH)
        return 0

    lax.fori_loop(1, 8, greet_mp, 0)

    def greet_back(i, _):
        @pl.when(jnp.logical_or(j != m, i != m))
        def _():
            pl.semaphore_signal(barrier, inc=1, device_id=(clip8 + m, i), device_id_type=MESH)

        return 0

    lax.fori_loop(0, 8, greet_back, 0)

    row, col = iota((128, 128), 0), iota((128, 128), 1)
    perm[...] = jnp.where((row >> 4 == (col & 7)) & ((row & 15) == col >> 3), 1.0, 0.0).astype(BF)
    row, col = iota((128, 512), 0), iota((128, 512), 1)
    hit = ((col >> 7) == ((row >> 2) & 3)) & (((col & 127) >> 2) == ((row >> 4) * 4 + (row & 3)))
    pool[...] = jnp.where(hit, 0.25, 0.0).astype(BF)
    tv[...] = jnp.where(iota((8, 128, 256), 2) == W, 1.0, 0.0).astype(BF)

    zh, y = m // 4, m % 4
    across = (m + 4) % 8

    def ring(k):
        return zh * 4 + (y + k) % 4

    def behind(k):
        return zh * 4 + (y + 4 - k) % 4

    def w_z():
        return pltpu.make_async_remote_copy(
            src_ref=wout_ref, dst_ref=wall.at[m], send_sem=ws_sem.at[0], recv_sem=wr_sem.at[0],
            device_id=(f, across), device_id_type=MESH,
        )

    def w_y(k):
        return pltpu.make_async_remote_copy(
            src_ref=wout_ref, dst_ref=wall.at[m], send_sem=ws_sem.at[k], recv_sem=wr_sem.at[k],
            device_id=(f, ring(k)), device_id_type=MESH,
        )

    def w_on(k):
        return pltpu.make_async_remote_copy(
            src_ref=wall.at[across], dst_ref=wall.at[across], send_sem=ws_sem.at[k], recv_sem=wr_sem.at[k],
            device_id=(f, ring(k)), device_id_type=MESH,
        )

    def w_pass(k, shard):
        return pltpu.make_async_remote_copy(
            src_ref=wall.at[shard], dst_ref=wall.at[shard], send_sem=wp_sem.at[k], recv_sem=wf_sem.at[k],
            device_id=(f + 1 - 2 * core, m), device_id_type=MESH,
        )

    def q_copy(i, half):
        to = mate(i % 8)
        chunk = (i // 8) * 2 + half
        return pltpu.make_async_remote_copy(
            src_ref=qsend.at[i, half], dst_ref=qrecv.at[chunk, j], send_sem=qs_sem.at[i, half],
            recv_sem=qr_sem.at[chunk, i % 8], device_id=(clip8 + to, m), device_id_type=MESH,
        )

    def q_own(i, half):
        chunk = (i // 8) * 2 + half
        return pltpu.make_async_copy(qsend.at[i, half], qrecv.at[chunk, j], qr_sem.at[chunk, 6])

    def q_start(i, half):
        @pl.when(i % 8 == 6)
        def _():
            q_own(i, half).start()

        @pl.when(i % 8 != 6)
        def _():
            q_copy(i, half).start()

    def normalize(slot, to):
        for n in range(8):
            v = norm_rows(xb[slot, 2 * n : 2 * n + 2].astype(F32).reshape(32, D), gain_ref[...].reshape(1, D))
            v = v.reshape(2, 2, 8, D)
            to[16 * n : 16 * n + 16, :] = v[:, 0].reshape(16, D).astype(BF)
            to[128 + 16 * n : 144 + 16 * n, :] = v[:, 1].reshape(16, D).astype(BF)

    def project(i, now, later, slot):
        @pl.when(i + 1 < 16)
        def _():
            x_copy(i + 1, slot).wait()

        qkv = lax.dot_general(wt_ref[...], now[...], NT, preferred_element_type=F32)
        qsend[i, 0] = qkv[:, :128].astype(BF)
        qsend[i, 1] = qkv[:, 128:].astype(BF)
        normalize(slot, later)

        @pl.when(i + 3 < 16)
        def _():
            x_copy(i + 3, slot).start()

    def two(n, _):
        project(2 * n, nb0, nb1, 1)
        project(2 * n + 1, nb1, nb0, 0)
        return 0

    def two_sent(n, _):
        two(n, 0)
        q_start(2 * n, 0)
        q_start(2 * n + 1, 0)
        return 0

    w_in(0).wait()
    x_copy(0, 0).wait()
    normalize(0, nb0)
    x_copy(2, 0).start()
    lax.fori_loop(0, 2, two, 0)
    w_in(1).wait()
    w_in(2).wait()

    @pl.when(j == m)
    def _():
        pl.semaphore_wait(barrier, 29)

    @pl.when(j != m)
    def _():
        pl.semaphore_wait(barrier, 30)

    def first(i, _):
        q_start(i, 0)
        return 0

    lax.fori_loop(0, 4, first, 0)

    @pl.when(core == 0)
    def _():
        for k in range(1, 4):
            w_y(k).start()

    @pl.when(core == 1)
    def _():
        w_z().start()

    def two_later(n, _):
        two(n, 0)
        q_start(2 * n - 8, 1)
        q_start(2 * n - 7, 1)
        return 0

    lax.fori_loop(2, 4, two_sent, 0)
    lax.fori_loop(4, 6, two_later, 0)

    @pl.when(core == 1)
    def _():
        w_z().wait()
        for k in range(1, 4):
            w_on(k).start()

    own_w = pltpu.make_async_copy(wout_ref, wall.at[m], wown_sem)
    own_w.start()
    for half in range(2):
        xs_copy(half).start()
    lax.fori_loop(6, 8, two_later, 0)

    def p_copy(chunk, i):
        to = (j + i) % 8
        rows = pl.ds(pl.multiple_of(chunk * 32, 32), 32)
        return pltpu.make_async_remote_copy(
            src_ref=psend.at[to, rows], dst_ref=arecv.at[m, rows], send_sem=ps_sem.at[chunk, i],
            recv_sem=pr_sem.at[chunk, m], device_id=(clip8 + to, j), device_id_type=MESH,
        )

    def p_own(chunk):
        rows = pl.ds(pl.multiple_of(chunk * 32, 32), 32)
        return pltpu.make_async_copy(psend.at[j, rows], arecv.at[m, rows], pr_sem.at[chunk, m])

    def attend(chunk, feed=None):
        def turn(i, _):
            pltpu.make_async_copy(qsend.at[0, 0], qrecv.at[chunk, source(i)], qr_sem.at[chunk, i]).wait()
            if feed is not None:
                q_start(8 + i, feed)
            s = source(i)
            block = qrecv.at[chunk, s]
            rows = pl.ds(pl.multiple_of(s * 16, 16), 16)
            for k, to in enumerate((tq, tk, tv)):
                part = lax.dot_general(perm[...], block[k * W : (k + 1) * W, :], NT, preferred_element_type=F32)
                to[:, rows, 0:W] = part.astype(BF).reshape(8, 16, W)
            return 0

        lax.fori_loop(0, 8, turn, 0)

        def quad(n, _):
            first = iota((128, W), 1) < HDIM
            wide = iota((128, 256), 1) < HDIM
            scale = math.log2(math.e) / math.sqrt(HDIM)
            for p in range(4):
                q = tq[4 * n + p]
                zero = jnp.zeros_like(q)
                q2 = jnp.concatenate([jnp.where(first, q, zero), jnp.where(first, zero, q)], axis=0)
                s = lax.dot_general(q2, tk[4 * n + p], NT, preferred_element_type=F32)
                top = jnp.max(s, axis=-1, keepdims=True)
                e = jnp.exp2((s - top) * scale).astype(BF)
                o = jnp.dot(e, tv[4 * n + p], preferred_element_type=F32)
                o = o * (1.0 / o[:, W : W + 1])
                att[p * 128 : (p + 1) * 128, :] = jnp.where(wide, o[:128], o[128:]).astype(BF)
            mean = jnp.dot(pool[...], att[...], preferred_element_type=F32).astype(BF)
            psend[:, pl.ds(pl.multiple_of(chunk * 32 + n * 16, 16), 16), :] = mean.reshape(8, 16, 256)
            return 0

        lax.fori_loop(0, 2, quad, 0)

        def back(i, _):
            here = jnp.logical_and(i == 0, j == m)

            @pl.when(here)
            def _():
                p_own(chunk).start()

            @pl.when(jnp.logical_not(here))
            def _():
                p_copy(chunk, i).start()

            return 0

        lax.fori_loop(0, 8, back, 0)

    def f_copy(chunk, e):
        owner = across if e > 3 else m
        rows = fin.at[owner, pl.ds(pl.multiple_of(chunk * 32, 32), 32)]
        return pltpu.make_async_remote_copy(
            src_ref=rows, dst_ref=rows, send_sem=fs_sem.at[chunk, e], recv_sem=fr_sem.at[chunk, e],
            device_id=(f, across if e == 0 else ring((e - 1) % 3 + 1)), device_id_type=MESH,
        )

    def pass_on(chunk):
        f_copy(chunk, 0).wait_recv()
        for e in range(4, 7):
            f_copy(chunk, e).start()

    def merge(chunk):
        rows = pl.ds(pl.multiple_of(chunk * 32, 32), 32)
        row, col = iota((32, 256), 0), iota((32, 256), 1)
        hit = ((col & 15) == (chunk % 2) * 8 + (row >> 2)) & ((col >> 6) == (row & 3))
        merged = jnp.dot(
            jnp.where(hit, 0.25, 0.0).astype(BF), xs[chunk // 2].reshape(256, D), preferred_element_type=F32
        )
        for s in range(8):
            pltpu.make_async_copy(psend.at[0, rows], arecv.at[s, rows], pr_sem.at[chunk, s]).wait()
        for s in range(8):
            merged += jnp.dot(arecv[s, rows, 0:W], wall[s], preferred_element_type=F32)
        fin[m, rows, :] = norm_rows(merged, pgain_ref[...].reshape(1, D)).astype(BF)

        for e in range(4):
            f_copy(chunk, e).start()

    def sort_rows():
        mine = slot_ref[pl.ds(pl.multiple_of(f * 8, 8), 8), :]
        parts = jnp.concatenate([mine >> 7, mine & 127], axis=0).astype(F32).astype(BF)
        lane, spot = iota((128, 1024), 0), iota((128, 1024), 1)
        patch = ((spot >> 5) & 3) * 32 + (spot >> 8) * 8 + ((spot >> 2) & 7)
        pick = jnp.where(patch == lane, 1.0, 0.0).astype(BF)
        picked = jnp.dot(parts, pick, preferred_element_type=F32)
        picked = picked[:8] * 128.0 + picked[8:]
        group, spot = iota((8, 1024), 0), iota((8, 1024), 1)
        keep = group == (spot & 3) * 2 + ((spot >> 7) & 1)
        along = jnp.sum(jnp.where(keep, picked, 0.0), axis=0, keepdims=True)
        same = jnp.where(iota((128, 128), 0) == iota((128, 128), 1), 1.0, 0.0).astype(BF)
        down = lax.dot_general(same, parts, NT, preferred_element_type=F32)
        down = down[:, :8] * 128.0 + down[:, 8:]
        count = jnp.zeros((128, 1024), F32)
        for n in range(8):
            count += jnp.where(down[:, n : n + 1] < along, 1.0, 0.0)
        rank = jnp.sum(count, axis=0, keepdims=True).astype(jnp.int32)

        def fill(n, _):
            rows = pl.ds(pl.multiple_of(n * 128, 128), 128)
            order[rows, :] = jnp.where(iota((128, 1024), 0) + n * 128 == rank, 1.0, 0.0).astype(BF)
            return 0

        lax.fori_loop(0, 8, fill, 0)

    def place_rows():
        def block(b, found):
            slots = slot_ref[pl.ds(pl.multiple_of(b * 8, 8), 8), :]
            high = (slots >> 7) - f * 8
            high = jnp.where((high >= 0) & (high < 8), high + b * 8, -1)
            low = slots & 127
            row = iota((128, 128), 0)
            highs = [jnp.where(high[n : n + 1] == row, 1.0, 0.0).astype(BF) for n in range(8)]
            lows = [jnp.where(low[n : n + 1] == row, 1.0, 0.0).astype(BF) for n in range(8)]
            return found + lax.dot_general(
                jnp.concatenate(lows, axis=1), jnp.concatenate(highs, axis=1), NT, preferred_element_type=F32
            )

        found = lax.fori_loop(0, 16, block, jnp.zeros((128, 128), F32))
        row, col = iota((128, 128), 0), iota((128, 128), 1)
        marks = found.astype(BF)
        before = jnp.where(row > col, 1.0, 0.0).astype(BF)
        rank = jnp.dot(before, marks, preferred_element_type=F32)
        sums = jnp.dot(jnp.ones((128, 128), BF), marks, preferred_element_type=F32).astype(BF)
        lower = jnp.where((row >> 3 == col >> 3) & (row < col), 1.0, 0.0).astype(BF)
        rank += jnp.dot(sums, lower, preferred_element_type=F32)
        key = found * (rank + ((col >> 3) * 64).astype(F32))
        for n in range(8):
            at = jnp.sum(jnp.where((col & 7) == n, key, 0.0), axis=1, keepdims=True).astype(jnp.int32)
            place[n * 128 : n * 128 + 128, :] = jnp.where(iota((128, 1024), 1) == at, 1.0, 0.0).astype(BF)

    sort_rows()
    place_rows()
    attend(0)

    own_w.wait()
    for half in range(2):
        xs_copy(half).wait()

    @pl.when(core == 0)
    def _():
        for k in range(1, 4):
            w_y(k).wait()
            w_pass(k, behind(k)).start()

    @pl.when(core == 1)
    def _():
        w_pass(0, across).start()
        for k in range(1, 4):
            w_on(k).wait()
            w_pass(k, (behind(k) + 4) % 8).start()

    attend(1, 0)

    @pl.when(core == 0)
    def _():
        for k in range(1, 4):
            w_pass(k, behind(k)).wait_send()
        w_pass(0, across).wait_recv()
        for k in range(1, 4):
            w_pass(k, (behind(k) + 4) % 8).wait_recv()

    @pl.when(core == 1)
    def _():
        w_pass(0, across).wait_send()
        for k in range(1, 4):
            w_pass(k, (behind(k) + 4) % 8).wait_send()
        for k in range(1, 4):
            w_pass(k, behind(k)).wait_recv()

    def read_out(chunk):
        f_rows = pl.ds(pl.multiple_of(chunk * 32, 32), 32)
        for e in range(1, 7):
            f_copy(chunk, e).wait_recv()
        rows = pl.ds(pl.multiple_of(chunk * 256, 256), 256)
        proj[rows, :] = jnp.dot(
            fin[:, f_rows, :].reshape(256, D), wllm_ref[...], preferred_element_type=F32
        ).astype(BF)

    merge(0)
    attend(2, 1)
    pass_on(0)
    merge(1)
    attend(3)
    merge(2)
    pass_on(1)
    merge(3)
    pass_on(2)
    read_out(0)
    pass_on(3)
    read_out(1)

    read_out(2)
    total[...] = jnp.dot(order[:, :768], proj[:768, :], preferred_element_type=F32)
    read_out(3)

    def o_copy(half, i):
        a, b, c = FAR[i]
        to = ((f // 8 + a) % 2) * 8 + ((cx + b) % 4) * 2 + (core + c) % 2
        return pltpu.make_async_remote_copy(
            src_ref=fsend.at[half, to], dst_ref=frecv.at[half, f], send_sem=os_sem.at[half, i],
            recv_sem=or_sem.at[half, i], device_id=(to, m), device_id_type=MESH,
        )

    for half in range(2):
        lanes = slice(half * 256, half * 256 + 256)
        turned = total[:, lanes] + jnp.dot(order[:, 768:], proj[768:, lanes], preferred_element_type=F32)
        fsend[half] = turned.astype(BF).reshape(16, 64, 256)
        for i in range(15):
            o_copy(half, i).start()
        frecv[half, f] = fsend[half, f]

    for half in range(2):
        for i in range(15):
            o_copy(half, i).wait_recv()
        out_ref[:, half * 256 : half * 256 + 256] = jnp.dot(
            place[...], frecv[half].reshape(1024, 256), preferred_element_type=F32
        ).astype(BF)

    def left_q(i, _):
        @pl.when(i % 8 != 6)
        def _():
            q_copy(i, 0).wait_send()
            q_copy(i, 1).wait_send()

        return 0

    lax.fori_loop(0, 16, left_q, 0)

    def left_p(i, _):
        @pl.when(jnp.logical_not(jnp.logical_and(i == 0, j == m)))
        def _():
            for chunk in range(CHUNKS):
                p_copy(chunk, i).wait_send()

        return 0

    lax.fori_loop(0, 8, left_p, 0)

    for chunk in range(CHUNKS):
        for e in range(7):
            f_copy(chunk, e).wait_send()
    for half in range(2):
        for i in range(15):
            o_copy(half, i).wait_send()


def per_device(stream, norm_gain, w_qkv, w_out, pool_gain, w_llm, owner_slot):
    frames = stream.reshape(16, 256, D)
    wt = jnp.swapaxes(w_qkv, 1, 2).reshape(3 * W, D)
    vmem, hbm = pl.BlockSpec(memory_space=pltpu.VMEM), pl.BlockSpec(memory_space=pl.ANY)
    dma = pltpu.SemaphoreType.DMA
    return pl.pallas_call(
        kernel,
        out_shape=jax.ShapeDtypeStruct((1024, 512), BF),
        in_specs=[hbm, vmem, hbm, hbm, vmem, hbm, vmem],
        out_specs=vmem,
        scratch_shapes=[
            pltpu.VMEM((3 * W, D), BF),
            pltpu.VMEM((W, D), BF),
            pltpu.VMEM((D, 512), BF),
            pltpu.VMEM((2, 16, 16, D), BF),
            pltpu.VMEM((256, D), BF),
            pltpu.VMEM((256, D), BF),
            pltpu.VMEM((16, 2, 3 * W, 128), BF),
            pltpu.VMEM((4, 8, 3 * W, 128), BF),
            pltpu.VMEM((8, 128, W), BF),
            pltpu.VMEM((8, 128, W), BF),
            pltpu.VMEM((8, 128, 256), BF),
            pltpu.VMEM((512, 256), BF),
            pltpu.VMEM((8, 128, 256), BF),
            pltpu.VMEM((8, 128, 256), BF),
            pltpu.VMEM((8, W, D), BF),
            pltpu.VMEM((2, 16, 16, D), BF),
            pltpu.VMEM((8, 128, D), BF),
            pltpu.VMEM((1024, 512), BF),
            pltpu.VMEM((1024, 512), F32),
            pltpu.VMEM((1024, 1024), BF),
            pltpu.VMEM((1024, 1024), BF),
            pltpu.VMEM((2, 16, 64, 256), BF),
            pltpu.VMEM((2, 16, 64, 256), BF),
            pltpu.VMEM((128, 128), BF),
            pltpu.VMEM((128, 512), BF),
            dma((3,)), dma((2,)), dma((2,)), dma((16, 2)), dma((4, 8)), dma((4, 8)), dma((4, 8)),
            dma((4,)), dma((4,)), dma((4,)), dma((4,)), dma, dma((4, 8)), dma((4, 8)), dma((2, 16)), dma((2, 16)),
        ],
        compiler_params=pltpu.CompilerParams(
            collective_id=0, has_side_effects=True, vmem_limit_bytes=56 * 2**20
        ),
        name="video_layer",
    )(frames, norm_gain, wt, w_out, pool_gain, w_llm, owner_slot.reshape(128, 128))


def solution(mesh):
    return jax.shard_map(
        per_device,
        mesh=mesh,
        in_specs=(
            P("frame", None), P(), P(None, None, "mp"), P("mp", None), P(), P(None, "mp"), P(),
        ),
        out_specs=P("frame", "mp"),
        check_vma=False,
    )
```

time: 150 us -> 114 us (0.76)
  Pallas kernels: 125 us -> 111 us
  between operations: 13.4 us -> 0.01 us
  local copies, waits for them, and re-layouts: 8.87 us -> 2.26 us
  other arithmetic: 1.84 us -> 0 us
    pallas_call x1, Pallas kernels: 125 us -> 111 us  [per_device(): pl.pallas_call(kernel, out_shape=jax.ShapeDtypeStruct((1024, 512), BF), i...]
    broadcast_in_dim x2 -> x0, local copies, waits for them, and re-layouts: 2.58 us -> none  [the longest x1 1.29 us: per_device(): norm_gain[None]]
where the time goes in v2:
time: 114 us
  Pallas kernels  111 us (97%)
  local copies, waits for them, and re-layouts  2.26 us (2%)
    pallas_call x1, Pallas kernels, per_device(): pl.pallas_call(kernel, out_shape=jax.ShapeDtypeStruct((1024, 512), BF), i...  111 us

profile of v2, /device:TPU:1, one launch (start us, length us, event | category | flops | bytes accessed | tf_op | source)
XLA Modules:
  0.0 113.5 jit_solution(15280157924108258279)
XLA Ops:
  0.0 111.2 %video_layer.1 = bf16[1024,512]{1,0:T(8,128)(2,1)} custom-call(bf16[16,256,1408]{2,1,0:T(8,128)(2,1)} %bitcast.5, f32[1408]{0:T(1024)} %gain_ref.1, bf16[528,1408]{1,0:T(8,128)(2,1)} %bitcast.6, bf16[176,1408]{1,0:T(8,128)(2,1)} %wout_hbm.1, f32[1408]{0:T(1024)} %pgain_ref.1, bf16[1408,512]{1,0:T(8,128)(2,1)} %wllm_hbm.1, s32[128,128]{1,0:T(8,128)} %bitcast.7), custom_call_target="tpu_custom_call" | custom-call | tf_op jit(solution)/shard_map/video_layer/pallas_call | solution.py:503
  111.3 2.3 %copy.9 = bf16[1024,512]{1,0:T(8,128)(2,1)} copy(bf16[1024,512]{1,0:T(8,128)(2,1)} %video_layer.1) | data formatting | bytes 2097152

commit v3 on v2

--- a/solution.py
+++ b/solution.py
@@ -299,17 +299,19 @@
         lax.fori_loop(0, 8, back, 0)
 
     def f_copy(chunk, e):
-        owner = across if e > 3 else m
+        owner = ring(2) if e == 5 else across if e > 3 else m
         rows = fin.at[owner, pl.ds(pl.multiple_of(chunk * 32, 32), 32)]
         return pltpu.make_async_remote_copy(
             src_ref=rows, dst_ref=rows, send_sem=fs_sem.at[chunk, e], recv_sem=fr_sem.at[chunk, e],
-            device_id=(f, across if e == 0 else ring((e - 1) % 3 + 1)), device_id_type=MESH,
+            device_id=(f, across if e in (0, 5) else ring((e - 1) % 3 + 1)), device_id_type=MESH,
         )
 
     def pass_on(chunk):
         f_copy(chunk, 0).wait_recv()
-        for e in range(4, 7):
-            f_copy(chunk, e).start()
+        f_copy(chunk, 4).start()
+        f_copy(chunk, 6).start()
+        f_copy(chunk, 2).wait_recv()
+        f_copy(chunk, 5).start()
 
     def merge(chunk):
         rows = pl.ds(pl.multiple_of(chunk * 32, 32), 32)
@@ -324,7 +326,7 @@
             merged += jnp.dot(arecv[s, rows, 0:W], wall[s], preferred_element_type=F32)
         fin[m, rows, :] = norm_rows(merged, pgain_ref[...].reshape(1, D)).astype(BF)
 
-        for e in range(4):
+        for e in (0, 2, 1, 3):
             f_copy(chunk, e).start()
 
     def sort_rows():
@@ -420,7 +422,7 @@
 
     def read_out(chunk):
         f_rows = pl.ds(pl.multiple_of(chunk * 32, 32), 32)
-        for e in range(1, 7):
+        for e in (1, 3, 4, 5, 6):
             f_copy(chunk, e).wait_recv()
         rows = pl.ds(pl.multiple_of(chunk * 256, 256), 256)
         proj[rows, :] = jnp.dot(

time: 114 us -> 108 us (0.947)
  Pallas kernels: 111 us -> 106 us
    pallas_call x1, Pallas kernels: 111 us -> 106 us  [per_device(): pl.pallas_call(kernel, out_shape=jax.ShapeDtypeStruct((1024, 512), BF), i...]
where the time goes in v3:
time: 108 us
  Pallas kernels  106 us (98%)
  local copies, waits for them, and re-layouts  2.26 us (2%)
    pallas_call x1, Pallas kernels, per_device(): pl.pallas_call(kernel, out_shape=jax.ShapeDtypeStruct((1024, 512), BF), i...  106 us
    unnamed x1, local copies, waits for them, and re-layouts  2.26 us

profile of v3, /device:TPU:1, one launch (start us, length us, event | category | flops | bytes accessed | tf_op | source)
XLA Modules:
  0.0 108.3 jit_solution(13569822929522838739)
XLA Ops:
  0.0 106.0 %video_layer.1 = bf16[1024,512]{1,0:T(8,128)(2,1)} custom-call(bf16[16,256,1408]{2,1,0:T(8,128)(2,1)} %bitcast.5, f32[1408]{0:T(1024)} %gain_ref.1, bf16[528,1408]{1,0:T(8,128)(2,1)} %bitcast.6, bf16[176,1408]{1,0:T(8,128)(2,1)} %wout_hbm.1, f32[1408]{0:T(1024)} %pgain_ref.1, bf16[1408,512]{1,0:T(8,128)(2,1)} %wllm_hbm.1, s32[128,128]{1,0:T(8,128)} %bitcast.7), custom_call_target="tpu_custom_call" | custom-call | tf_op jit(solution)/shard_map/video_layer/pallas_call | solution.py:505
  106.0 2.3 %copy.9 = bf16[1024,512]{1,0:T(8,128)(2,1)} copy(bf16[1024,512]{1,0:T(8,128)(2,1)} %video_layer.1) | data formatting | bytes 2097152

commit v4 on v3

--- a/solution.py
+++ b/solution.py
@@ -381,8 +381,6 @@
             at = jnp.sum(jnp.where((col & 7) == n, key, 0.0), axis=1, keepdims=True).astype(jnp.int32)
             place[n * 128 : n * 128 + 128, :] = jnp.where(iota((128, 1024), 1) == at, 1.0, 0.0).astype(BF)
 
-    sort_rows()
-    place_rows()
     attend(0)
 
     own_w.wait()
@@ -433,14 +431,16 @@
     attend(2, 1)
     pass_on(0)
     merge(1)
+    sort_rows()
+    place_rows()
+    pass_on(1)
     attend(3)
     merge(2)
-    pass_on(1)
+    pass_on(2)
     merge(3)
-    pass_on(2)
     read_out(0)
+    read_out(1)
     pass_on(3)
-    read_out(1)
 
     read_out(2)
     total[...] = jnp.dot(order[:, :768], proj[:768, :], preferred_element_type=F32)

time: 108 us -> 106 us (0.981)
  Pallas kernels: 106 us -> 104 us
    pallas_call x1, Pallas kernels: 106 us -> 104 us  [per_device(): pl.pallas_call(kernel, out_shape=jax.ShapeDtypeStruct((1024, 512), BF), i...]
where the time goes in v4:
time: 106 us
  Pallas kernels  104 us (98%)
  local copies, waits for them, and re-layouts  2.26 us (2%)
    pallas_call x1, Pallas kernels, per_device(): pl.pallas_call(kernel, out_shape=jax.ShapeDtypeStruct((1024, 512), BF), i...  104 us
    unnamed x1, local copies, waits for them, and re-layouts  2.26 us

profile of v4, /device:TPU:1, one launch (start us, length us, event | category | flops | bytes accessed | tf_op | source)
XLA Modules:
  0.0 106.2 jit_solution(6456911439007054293)
XLA Ops:
  0.0 103.9 %video_layer.1 = bf16[1024,512]{1,0:T(8,128)(2,1)} custom-call(bf16[16,256,1408]{2,1,0:T(8,128)(2,1)} %bitcast.5, f32[1408]{0:T(1024)} %gain_ref.1, bf16[528,1408]{1,0:T(8,128)(2,1)} %bitcast.6, bf16[176,1408]{1,0:T(8,128)(2,1)} %wout_hbm.1, f32[1408]{0:T(1024)} %pgain_ref.1, bf16[1408,512]{1,0:T(8,128)(2,1)} %wllm_hbm.1, s32[128,128]{1,0:T(8,128)} %bitcast.7), custom_call_target="tpu_custom_call" | custom-call | tf_op jit(solution)/shard_map/video_layer/pallas_call | solution.py:505
  103.9 2.3 %copy.9 = bf16[1024,512]{1,0:T(8,128)(2,1)} copy(bf16[1024,512]{1,0:T(8,128)(2,1)} %video_layer.1) | data formatting | bytes 2097152

commit v5 on v4

--- a/solution.py
+++ b/solution.py
@@ -433,8 +433,8 @@
     merge(1)
     sort_rows()
     place_rows()
+    attend(3)
     pass_on(1)
-    attend(3)
     merge(2)
     pass_on(2)
     merge(3)

time: 106 us -> 107 us (level)
  no operation moved by 1% of the time
where the time goes in v5:
time: 107 us
  Pallas kernels  104 us (97%)
  local copies, waits for them, and re-layouts  2.26 us (2%)
    pallas_call x1, Pallas kernels, per_device(): pl.pallas_call(kernel, out_shape=jax.ShapeDtypeStruct((1024, 512), BF), i...  104 us
    unnamed x1, local copies, waits for them, and re-layouts  2.26 us

profile of v5, /device:TPU:1, one launch (start us, length us, event | category | flops | bytes accessed | tf_op | source)
XLA Modules:
  0.0 106.7 jit_solution(10538663790023198846)
XLA Ops:
  0.0 104.4 %video_layer.1 = bf16[1024,512]{1,0:T(8,128)(2,1)} custom-call(bf16[16,256,1408]{2,1,0:T(8,128)(2,1)} %bitcast.5, f32[1408]{0:T(1024)} %gain_ref.1, bf16[528,1408]{1,0:T(8,128)(2,1)} %bitcast.6, bf16[176,1408]{1,0:T(8,128)(2,1)} %wout_hbm.1, f32[1408]{0:T(1024)} %pgain_ref.1, bf16[1408,512]{1,0:T(8,128)(2,1)} %wllm_hbm.1, s32[128,128]{1,0:T(8,128)} %bitcast.7), custom_call_target="tpu_custom_call" | custom-call | tf_op jit(solution)/shard_map/video_layer/pallas_call | solution.py:505
  104.4 2.3 %copy.9 = bf16[1024,512]{1,0:T(8,128)(2,1)} copy(bf16[1024,512]{1,0:T(8,128)(2,1)} %video_layer.1) | data formatting | bytes 2097152
